TPU v7x, 128 devices: a whole 4x4x4 slice. The times are simulated.
128 devices in a mesh: scene: 8 (over y, core), frame: 16 (over z, x).
Axes of the slice: x: 4, y: 4, z: 4, core: 2. Of those that a mesh axis runs over, the one named last changes fastest.
Arguments:
- occupancy: bfloat16 [8, 64, 64, 2048], P('scene', 'frame'), may hold values from -6 to 6
- scene_lengths: int32 [8], P('scene'), may hold values from 8 to 64, as said below
- conv1_weight: bfloat16 [128, 1728], replicated, may hold values from -0.15625 to 0.15625
- conv2_weight: bfloat16 [256, 3456], replicated, may hold values from -0.109375 to 0.109375
- temporal_weight: bfloat16 [3, 256, 256], replicated, may hold values from -0.21875 to 0.21875
- query_weight: bfloat16 [256, 256], replicated
- key_weight: bfloat16 [256, 256], replicated
- value_weight: bfloat16 [256, 256], replicated, may hold values from -0.375 to 0.375
- out_weight: bfloat16 [256, 256], replicated, may hold values from -0.375 to 0.375
Outputs:
- encoded: bfloat16 [8, 64, 256, 512], P('scene', 'frame')
- kl_loss: float32 [], replicated
Inputs may be any that keep to these rules, and one draw needn't show every extreme that they name: `scene_lengths`: non-decreasing along the scenes; the first scene has exactly 8 frames with data and the last exactly 64.
All inputs are finite; a program needn't handle non-finite values.
Results may differ from a plain program's by a relative error of at most 0.011.
Values may be sent and summed in bfloat16 or wider, within the bound.
A program may use at most 192 MiB of HBM per device.

v0:
```python
import jax
import jax.numpy as jnp
from jax import lax
from jax.sharding import PartitionSpec as P

CIN = 64
C1 = 128
C2 = 256
HEADS = 4
HD = 64
HI = 16
ZD = 8
CELLS = 512
NORM_EPS = 1e-06


def extended(cells, sides, width):
    for axis, dim in sides:
        count = lax.axis_size(axis)
        ends = count - 1
        head = lax.slice_in_dim(cells, 0, width, axis=dim)
        tail = lax.slice_in_dim(cells, cells.shape[dim] - width, cells.shape[dim], axis=dim)
        cells = jnp.concatenate(
            [
                lax.ppermute(tail, axis, [(i, (i + 1) % count) for i in range(ends)]),
                cells,
                lax.ppermute(head, axis, [((i + 1) % count, i) for i in range(ends)]),
            ],
            axis=dim,
        )
    return cells


def spatial_conv(voxels, weight, channels_in, stride):
    channels_out = weight.shape[0]
    kernel = weight.reshape(channels_out, channels_in, 3, 3, 3)
    return lax.conv_general_dilated(
        voxels,
        kernel,
        (stride, stride, 1),
        ((1, 1), (1, 1), (1, 1)),
        dimension_numbers=("NCDHW", "OIDHW", "NCDHW"),
        preferred_element_type=jnp.float32,
    )


def mix_channels(weight, maps):
    return jnp.einsum("oc,fcn->fon", weight, maps, preferred_element_type=jnp.float32)


def temporal_block(padded, second_maps, temporal_weight):
    count_frames = second_maps.shape[0]
    temporal_sum = mix_channels(temporal_weight[0], padded[0:count_frames])
    for tap in range(1, 3):
        temporal_sum = temporal_sum + mix_channels(
            temporal_weight[tap], padded[tap : tap + count_frames]
        )
    residual_maps = (second_maps.astype(jnp.float32) + jax.nn.silu(temporal_sum)).astype(
        jnp.bfloat16
    )
    return residual_maps.astype(jnp.float32)


def project_rows(residual_f, query_weight, key_weight, value_weight):
    count_frames = residual_f.shape[0]
    count_cells = residual_f.shape[2]
    normed = (
        residual_f * lax.rsqrt(jnp.mean(residual_f * residual_f, axis=1, keepdims=True) + NORM_EPS)
    ).astype(jnp.bfloat16)
    queries = (
        mix_channels(query_weight, normed)
        .astype(jnp.bfloat16)
        .reshape(count_frames, HEADS, HD, count_cells)
    )
    key_rows = (
        mix_channels(key_weight, normed)
        .astype(jnp.bfloat16)
        .reshape(count_frames, HEADS, HD, count_cells)
    )
    value_rows = (
        mix_channels(value_weight, normed)
        .astype(jnp.bfloat16)
        .reshape(count_frames, HEADS, HD, count_cells)
    )
    return (queries, key_rows, value_rows)


def finish_rows(residual_f, attended, out_weight, valid_rows):
    count_frames = residual_f.shape[0]
    count_cells = residual_f.shape[2]
    out_full = residual_f + mix_channels(
        out_weight, attended.reshape(count_frames, C2, count_cells)
    )
    return (out_full * valid_rows[:, None, None]).astype(jnp.bfloat16)


def shards(
    occupancy,
    scene_lengths,
    conv1_weight,
    conv2_weight,
    temporal_weight,
    query_weight,
    key_weight,
    value_weight,
    out_weight,
):
    f_dev = occupancy.shape[1]
    length = scene_lengths[0]
    first_frame = lax.axis_index("frame") * f_dev
    frame_ids = first_frame + jnp.arange(f_dev, dtype=jnp.int32)
    valid_rows = (frame_ids < length).astype(jnp.float32)
    voxels = occupancy[0].reshape(f_dev, CIN, HI, HI, ZD)
    first_maps = jax.nn.silu(spatial_conv(voxels, conv1_weight, CIN, 2)).astype(jnp.bfloat16)
    second_full = jax.nn.silu(spatial_conv(first_maps, conv2_weight, C1, 1))
    second_maps = (second_full.reshape(f_dev, C2, CELLS) * valid_rows[:, None, None]).astype(
        jnp.bfloat16
    )
    padded = extended(second_maps, (("frame", 0),), 1)
    residual_f = temporal_block(padded, second_maps, temporal_weight)
    queries, key_rows, value_rows = project_rows(residual_f, query_weight, key_weight, value_weight)
    running_max = jnp.full((f_dev, HEADS, CELLS), -1e30, jnp.float32)
    panel_keys = lax.all_gather(key_rows, "frame", axis=0, tiled=True)
    panel_values = lax.all_gather(value_rows, "frame", axis=0, tiled=True)
    count_keys = panel_keys.shape[0]
    scores = jnp.einsum(
        "qhdc,khdc->qkhc", queries, panel_keys, preferred_element_type=jnp.float32
    ) * HD ** (-0.5)
    key_mask = (jnp.arange(count_keys) < length)[None, :, None, None]
    scores = jnp.where(key_mask, scores, -1e30)
    new_max = jnp.maximum(running_max, jnp.max(scores, axis=1))
    raw_weights = jnp.where(key_mask, jnp.exp(scores - new_max[:, None]), 0.0)
    new_sum = jnp.sum(raw_weights, axis=1)
    addition = jnp.einsum(
        "qkhc,khdc->qhdc",
        raw_weights.astype(jnp.bfloat16),
        panel_values,
        preferred_element_type=jnp.float32,
    )
    attended = (addition / new_sum[:, :, None, :]).astype(jnp.bfloat16)
    encoded = finish_rows(residual_f, attended, out_weight, valid_rows)
    squares = jnp.sum(jnp.square(encoded.astype(jnp.float32)))
    grand_total = lax.psum(squares, ("scene", "frame"))
    slot_count = float(lax.axis_size("scene") * lax.axis_size("frame") * f_dev * CELLS * C2)
    kl_loss = 0.5 * grand_total / slot_count
    return (encoded[None], kl_loss)


def solution(mesh):
    placed = (P("scene", "frame", None, None), P("scene"), P(), P(), P(), P(), P(), P(), P())
    return jax.shard_map(
        shards,
        mesh=mesh,
        in_specs=placed,
        out_specs=(P("scene", "frame", None, None), P()),
        check_vma=False,
    )
```

profile of v0, /device:TPU:1, one launch (start us, length us, event | category | flops | bytes accessed | tf_op | source)
XLA Modules:
  0.0 420.5 jit_solution(17460069256639030074)
XLA Ops:
  7.2 0.0 copy-start
  7.2 0.0 all-gather.5.cloned.1.call-start
  7.9 2.6 copy.62
  10.5 0.0 copy-start.3
  10.6 2.9 reshape.49
  13.4 0.0 copy-done.3
  13.4 1.1 copy.59
  14.5 1.5 reshape.48
  16.0 0.0 copy-start.1
  16.0 5.0 %fusion.28 = bf16[4,128,8,8,8]{1,0,4,3,2:T(4,128)(2,1)S(1)} fusion(bf16[4,64,16,16,8]{1,4,3,2,0:T(8,128)(2,1)S(1)} %bitcast.90, bf16[128,64,3,3,3]{0,4,3,2,1:T(4,128)(2,1)S(1)} %reshape.48), kind=kOutput, calls=%fused_computation.44 | convolution fusion | flops 764018688 | bytes 2015232 | tf_op jit(solution)/shard_map/conv_general_dilated | solution.py:37
  21.0 0.0 copy-done.1
  21.0 7.9 %multiply_convert_fusion = (bf16[4,256,8,8,8]{1,0,4,3,2:T(4,128)(2,1)S(1)}, f32[4,256,8,8,8]{1,0,4,3,2:T(4,128)}) fusion(f32[4]{0:T(128)S(1)} %compare_convert_fusion, bf16[4,128,8,8,8]{1,0,4,3,2:T(4,128)(2,1)S(1)} %fusion.28, bf16[256,128,3,3,3]{0,4,3,2,1:T(4,128)(2,1)S(1)} %copy-done.1), kind=kOutput, calls=%fused_computation.24 | convolution fusion | flops 2794455040 | bytes 5439504 | tf_op jit(solution)/shard_map/conv_general_dilated | solution.py:37
  28.9 1.9 copy.64
  30.8 0.0 copy-start.4
  30.8 0.3 multiply_convert_fusion.1
  31.2 4.0 collective-permute-start
  35.1 1.5 collective-permute-start.1
  36.6 0.0 copy-done.4
  36.6 0.5 fusion.26
  37.1 3.0 collective-permute-done
  40.1 0.4 fusion.24
  40.5 0.0 copy-start.5
  40.5 3.4 collective-permute-done.1
  43.9 1.1 fusion.2
  44.9 0.0 copy-start.6
  45.0 0.0 copy-done.5
  45.0 1.4 convolution_convert_fusion.1
  46.4 0.0 all-gather.5.cloned.1.call-update
  46.4 0.0 all-gather.3.cloned.1.call-start
  46.5 0.0 copy-done.6
  46.5 1.4 convolution_convert_fusion.2
  47.9 0.0 all-gather.3.cloned.1.call-update
  48.0 0.5 convolution_convert_fusion
  48.4 2.5 copy.67
  50.9 112.4 %all-gather.5.cloned.1.call-done = bf16[64,4,64,512]{3,2,1,0:T(8,128)(2,1)} async-done(((bf16[4,4,64,512]{3,2,1,0:T(8,128)(2,1)}), bf16[64,4,64,512]{3,2,1,0:T(8,128)(2,1)}) %all-gather.5.cloned.1.call-update) | async-done | bytes 16777232 | tf_op jit(solution)/shard_map/all_gather | solution.py:123
  163.3 46.8 %copy.66 = bf16[64,4,64,512]{2,0,3,1:T(8,128)(2,1)} copy(bf16[64,4,64,512]{3,2,1,0:T(8,128)(2,1)} %all-gather.5.cloned.1.call-done) | data formatting | bytes 33554432 | tf_op jit(solution)/shard_map/all_gather | solution.py:123
  210.1 24.4 %bitcast_reduce_fusion = (f32[4,4,512]{0,2,1:T(8,128)}, f32[4,512,64,4]{2,3,1,0:T(4,128)}) fusion(pred[64]{0:T(512)(128)(4,1)S(1)} %iota_compare_fusion, bf16[64,4,64,512]{2,0,3,1:T(8,128)(2,1)} %copy.66, bf16[4,4,64,512]{2,0,3,1:T(4,128)(2,1)S(1)} %copy-done.2), kind=kOutput, calls=%fused_computation.1 | convolution fusion | flops 68673536 | bytes 19955776 | tf_op jit(solution)/shard_map/qhdc,khdc->qkhc/dot_general | solution.py:126
  234.5 1.4 broadcast_maximum_fusion
  235.9 30.0 %fusion.20 = f32[4,4,512]{0,2,1:T(8,128)S(1)} fusion(f32[4,4,512]{0,2,1:T(8,128)S(1)} %broadcast_maximum_fusion, f32[4,512,64,4]{2,3,1,0:T(4,128)} %get-tuple-element.9, pred[64]{0:T(512)(128)(4,1)S(1)} %iota_compare_fusion), kind=kLoop, calls=%fused_computation.34 | loop fusion | flops 2613248 | bytes 2162752 | tf_op jit(solution)/shard_map/reduce_sum | solution.py:133
  265.9 0.3 copy.70
  266.2 10.9 %all-gather.3.cloned.1.call-done = bf16[64,4,64,512]{3,2,1,0:T(8,128)(2,1)} async-done(((bf16[4,4,64,512]{3,2,1,0:T(8,128)(2,1)}), bf16[64,4,64,512]{3,2,1,0:T(8,128)(2,1)}) %all-gather.3.cloned.1.call-update) | async-done | bytes 16777232 | tf_op jit(solution)/shard_map/all_gather | solution.py:124
  277.1 46.6 %copy.68 = bf16[64,4,64,512]{2,0,3,1:T(8,128)(2,1)} copy(bf16[64,4,64,512]{3,2,1,0:T(8,128)(2,1)} %all-gather.3.cloned.1.call-done) | data formatting | bytes 33554432 | tf_op jit(solution)/shard_map/all_gather | solution.py:124
  323.7 17.5 %fusion.11 = f32[4,512,64,4]{2,3,1,0:T(4,128)} fusion(bf16[64,4,64,512]{2,0,3,1:T(8,128)(2,1)} %copy.68, f32[4,512,64,4]{2,3,1,0:T(4,128)} %get-tuple-element.9, f32[4,4,512]{0,2,1:T(8,128)S(1)} %broadcast_maximum_fusion, pred[64]{0:T(512)(128)(4,1)S(1)} %iota_compare_fusion), kind=kOutput, calls=%fused_computation.22 | convolution fusion | flops 69730304 | bytes 21004352 | tf_op jit(solution)/shard_map/qkhc,khdc->qhdc/dot_general | solution.py:134
  341.2 3.5 copy.69
  344.7 0.3 fusion.6
  345.0 0.0 copy-done
  345.0 2.3 multiply_reduce_fusion
  347.3 64.6 %psum.7 = f32[]{:T(128)} all-reduce(f32[]{:T(128)} %get-tuple-element.10), channel_id=1, replica_groups=mesh['scene'=8,'frame'=16] {'scene','frame'}, use_global_device_ids=true, to_apply=%region_4.5 | all-reduce | flops 1 | bytes 8 | tf_op jit(solution)/shard_map/psum | solution.py:143
  (8 shorter events, 0.1 us)
Async XLA Ops:
  7.2 337.9 %copy-start = (bf16[256,256]{1,0:T(8,128)(2,1)S(1)}, bf16[256,256]{1,0:T(8,128)(2,1)}, u32[]{:S(2)}) copy-start(bf16[256,256]{1,0:T(8,128)(2,1)} %param.17) | copy-start | bytes 393220
  7.2 156.1 %all-gather.5.cloned.1.call-start = ((), (), s32[]{:S(2)}) async-start(), calls=%async_computation.1 | async-start | bytes 17825792 | tf_op jit(solution)/shard_map/all_gather | solution.py:123
  10.5 2.9 copy-start.3
  16.0 5.0 %copy-start.1 = (bf16[256,128,3,3,3]{0,4,3,2,1:T(4,128)(2,1)S(1)}, bf16[256,128,3,3,3]{0,4,3,2,1:T(4,128)(2,1)}, u32[]{:S(2)}) copy-start(bf16[256,128,3,3,3]{0,4,3,2,1:T(4,128)(2,1)} %reshape.49) | copy-start | bytes 5308420
  30.8 5.8 %copy-start.4 = (bf16[3,256,256]{2,1,0:T(8,128)(2,1)S(1)}, bf16[3,256,256]{2,1,0:T(8,128)(2,1)}, u32[]{:S(2)}) copy-start(bf16[3,256,256]{2,1,0:T(8,128)(2,1)} %param.13) | copy-start | bytes 1179652
  31.2 8.9 %collective-permute-start = (bf16[1,256,512]{2,1,0:T(8,128)(2,1)S(1)}, bf16[1,256,512]{2,1,0:T(8,128)(2,1)S(1)}, u32[]{:S(2)}, u32[]{:S(2)}) collective-permute-start(bf16[1,256,512]{2,1,0:T(8,128)(2,1)S(1)} %get-tuple-element.3), channel_id=1, source_target_pairs={{0,1},{1,2},{2,3},{3,4},{4,5},{5,6},{6,7},{7,8},{8,9},{9,10},{10,1... | collective-permute-start | bytes 786440 | tf_op jit(solution)/shard_map/ppermute | solution.py:25
  35.1 8.7 %collective-permute-start.1 = (bf16[1,256,512]{2,1,0:T(8,128)(2,1)S(1)}, bf16[1,256,512]{2,1,0:T(8,128)(2,1)S(1)}, u32[]{:S(2)}, u32[]{:S(2)}) collective-permute-start(bf16[1,256,512]{2,1,0:T(8,128)(2,1)S(1)} %get-tuple-element.2), channel_id=1, source_target_pairs={{1,0},{2,1},{3,2},{4,3},{5,4},{6,5},{7,6},{8,7},{9,8},{10,9},{11,1... | collective-permute-start | bytes 786440 | tf_op jit(solution)/shard_map/ppermute | solution.py:27
  40.5 4.5 %copy-start.5 = (bf16[256,256]{1,0:T(8,128)(2,1)S(1)}, bf16[256,256]{1,0:T(8,128)(2,1)}, u32[]{:S(2)}) copy-start(bf16[256,256]{1,0:T(8,128)(2,1)} %param.15) | copy-start | bytes 393220
  44.9 1.5 copy-start.6
  46.4 1.6 copy-start.7
  46.4 230.7 %all-gather.3.cloned.1.call-start = ((), (), s32[]{:S(2)}) async-start(), calls=%async_computation | async-start | bytes 17825792 | tf_op jit(solution)/shard_map/all_gather | solution.py:124
  50.9 159.2 %copy-start.2 = (bf16[4,4,64,512]{2,0,3,1:T(4,128)(2,1)S(1)}, bf16[4,4,64,512]{2,0,3,1:T(4,128)(2,1)}, u32[]{:S(2)}) copy-start(bf16[4,4,64,512]{2,0,3,1:T(4,128)(2,1)} %copy.67) | copy-start | bytes 3145732
Sparse Core Ops, SparseCore 0:
  46.6 116.7 all-gather.4
  166.0 111.0 all-gather.2
where the time goes:
time: 423 us; the launch traced here: 421 us
  waiting for transfers between devices  130 us (31%)
  local copies, waits for them, and re-layouts  110 us (26%)
  blocking collectives  64.6 us (15%)
  matrix products  62.2 us (15%)
  other arithmetic  32 us (8%)
  between operations  16.7 us (4%)
  starting transfers between devices  5.51 us (1%)
    all_gather x1, waiting for transfers between devices, shards(): panel_keys = lax.all_gather(key_rows, 'frame', axis=0, tiled=True)  112 us
    psum x1, blocking collectives, shards(): grand_total = lax.psum(squares, ('scene', 'frame'))  64.6 us
    all_gather x1, local copies, waits for them, and re-layouts, shards(): panel_keys = lax.all_gather(key_rows, 'frame', axis=0, tiled=True)  46.8 us
    all_gather x1, local copies, waits for them, and re-layouts, shards(): panel_values = lax.all_gather(value_rows, 'frame', axis=0, tiled=True)  46.6 us
    reduce_sum x1, other arithmetic, shards(): new_sum = jnp.sum(raw_weights, axis=1)  30 us
    dot_general x1, matrix products, shards(): jnp.einsum('qhdc,khdc->qkhc', queries, panel_keys, preferred_element_type...  24.4 us
    dot_general x1, matrix products, shards(): jnp.einsum('qkhc,khdc->qhdc', raw_weights.astype(jnp.bfloat16), panel_val...  17.5 us
    conv_general_dilated x2, matrix products, spatial_conv(): lax.conv_general_dilated(voxels, kernel, (stride, stride, 1), ((1, 1), (1...  12.8 us
  transfers between devices with their start and end apart: 4, of which 4 were waited for; matrix products, arithmetic and copies ran while one was open for 26% of the time, Pallas kernels for 0%

commit v1 on v0

--- a/solution.py
+++ b/solution.py
@@ -120,8 +120,13 @@
     residual_f = temporal_block(padded, second_maps, temporal_weight)
     queries, key_rows, value_rows = project_rows(residual_f, query_weight, key_weight, value_weight)
     running_max = jnp.full((f_dev, HEADS, CELLS), -1e30, jnp.float32)
-    panel_keys = lax.all_gather(key_rows, "frame", axis=0, tiled=True)
-    panel_values = lax.all_gather(value_rows, "frame", axis=0, tiled=True)
+    panel_keys, panel_values = jnp.split(
+        lax.all_gather(
+            jnp.concatenate([key_rows, value_rows], axis=1), "frame", axis=0, tiled=True
+        ),
+        [key_rows.shape[1]],
+        axis=1,
+    )
     count_keys = panel_keys.shape[0]
     scores = jnp.einsum(
         "qhdc,khdc->qkhc", queries, panel_keys, preferred_element_type=jnp.float32

time: 423 us -> 523 us (1.24)
  waiting for transfers between devices: 130 us -> 205 us
  local copies, waits for them, and re-layouts: 110 us -> 134 us
    unnamed x18 -> x20, local copies, waits for them, and re-layouts: 3.74 us -> 98.5 us
    all_gather x2 -> x0, local copies, waits for them, and re-layouts: 93.4 us -> none  [the longest x1 46.8 us: shards(): panel_keys = lax.all_gather(key_rows, 'frame', axis=0, tiled=True)]
    all_gather x2 -> x1, waiting for transfers between devices: 123 us -> 199 us  [shards(): lax.all_gather(jnp.concatenate([key_rows, value_rows], axis=1), 'frame',...]
    split x0 -> x1, local copies, waits for them, and re-layouts: none -> 23.2 us  [shards(): jnp.split(lax.all_gather(jnp.concatenate([key_rows, value_rows], axis=1),...]
  transfers between devices with their start and end apart: 4 -> 3, of which waited for: 4 -> 3; matrix products, arithmetic and copies ran while one was open for 26% -> 1% of each run, Pallas kernels for 0% -> 0%
where the time goes in v1:
time: 523 us; the launch traced here: 520 us
  waiting for transfers between devices  205 us (39%)
  local copies, waits for them, and re-layouts  134 us (26%)
  blocking collectives  64.6 us (12%)
  matrix products  60.2 us (12%)
  other arithmetic  33.5 us (6%)
  between operations  16.7 us (3%)
  starting transfers between devices  5.47 us (1%)
    all_gather x1, waiting for transfers between devices, shards(): lax.all_gather(jnp.concatenate([key_rows, value_rows], axis=1), 'frame',...  199 us
    unnamed x20, local copies, waits for them, and re-layouts  98.5 us
    psum x1, blocking collectives, shards(): grand_total = lax.psum(squares, ('scene', 'frame'))  64.6 us
    reduce_sum x1, other arithmetic, shards(): new_sum = jnp.sum(raw_weights, axis=1)  30 us
    dot_general x1, matrix products, shards(): jnp.einsum('qhdc,khdc->qkhc', queries, panel_keys, preferred_element_type...  24.3 us
    split x1, local copies, waits for them, and re-layouts, shards(): jnp.split(lax.all_gather(jnp.concatenate([key_rows, value_rows], axis=1),...  23.2 us
    dot_general x1, matrix products, shards(): jnp.einsum('qkhc,khdc->qhdc', raw_weights.astype(jnp.bfloat16), panel_val...  17.5 us
    conv_general_dilated x2, matrix products, spatial_conv(): lax.conv_general_dilated(voxels, kernel, (stride, stride, 1), ((1, 1), (1...  12.8 us
  transfers between devices with their start and end apart: 3, of which 3 were waited for; matrix products, arithmetic and copies ran while one was open for 1% of the time, Pallas kernels for 0%

profile of v1, /device:TPU:1, one launch (start us, length us, event | category | flops | bytes accessed | tf_op | source)
XLA Modules:
  0.0 520.0 jit_solution(2546201668638889079)
XLA Ops:
  7.2 0.0 copy-start
  7.2 0.0 all-gather.2.cloned.1.call-start
  7.9 2.6 copy.62
  10.5 0.0 copy-start.3
  10.6 2.9 reshape.49
  13.4 0.0 copy-done.3
  13.4 1.1 copy.59
  14.5 1.5 reshape.48
  16.0 0.0 copy-start.1
  16.0 5.0 fusion.28
  21.0 0.0 copy-done.1
  21.0 7.8 %multiply_convert_fusion = (bf16[4,256,8,8,8]{1,0,4,3,2:T(4,128)(2,1)S(1)}, f32[4,256,8,8,8]{1,0,4,3,2:T(4,128)}) fusion(f32[4]{0:T(128)S(1)} %compare_convert_fusion, bf16[4,128,8,8,8]{1,0,4,3,2:T(4,128)(2,1)S(1)} %fusion.28, bf16[256,128,3,3,3]{0,4,3,2,1:T(4,128)(2,1)S(1)} %copy-done.1), kind=kOutput, calls=%fused_computation.25 | convolution fusion | flops 2794455040 | bytes 5439504 | tf_op jit(solution)/shard_map/conv_general_dilated | solution.py:37
  28.8 1.9 copy.64
  30.8 0.0 copy-start.4
  30.8 0.3 multiply_convert_fusion.1
  31.2 4.0 collective-permute-start
  35.1 1.5 collective-permute-start.1
  36.6 0.0 copy-done.4
  36.6 0.5 fusion.26
  37.1 3.0 collective-permute-done
  40.1 0.4 fusion.24
  40.5 0.0 copy-start.5
  40.5 3.4 collective-permute-done.1
  43.9 1.1 fusion.2
  44.9 0.0 copy-start.6
  45.0 0.0 copy-done.5
  45.0 0.5 convolution_convert_fusion.2
  45.4 0.4 copy-done.6
  45.8 0.5 convolution_convert_fusion.1
  46.3 1.5 pad_maximum_fusion
  47.8 0.0 all-gather.2.cloned.1.call-update
  47.9 0.9 copy-done.7
  48.7 0.5 convolution_convert_fusion
  49.2 2.5 copy.68
  51.7 198.8 %all-gather.2.cloned.1.call-done = bf16[64,8,64,512]{3,2,1,0:T(8,128)(2,1)} async-done(((bf16[4,8,64,512]{3,2,1,0:T(8,128)(2,1)}), bf16[64,8,64,512]{3,2,1,0:T(8,128)(2,1)}) %all-gather.2.cloned.1.call-update) | async-done | bytes 33554448 | tf_op jit(solution)/shard_map/all_gather | solution.py:124
  250.5 23.2 %fusion.50 = (bf16[64,4,64,512]{3,2,1,0:T(8,128)(2,1)}, bf16[64,4,64,512]{3,2,1,0:T(8,128)(2,1)}) fusion(bf16[64,8,64,512]{3,2,1,0:T(8,128)(2,1)} %all-gather.2.cloned.1.call-done), kind=kLoop, calls=%fused_computation.66 | loop fusion | bytes 67108864 | tf_op jit(solution)/shard_map/split | solution.py:123
  273.7 46.8 %copy.76 = bf16[64,4,64,512]{2,0,3,1:T(8,128)(2,1)} copy(bf16[64,4,64,512]{3,2,1,0:T(8,128)(2,1)} %get-tuple-element.2) | data formatting | bytes 33554432
  320.5 0.0 copy-done.2
  320.5 24.3 %bitcast_reduce_fusion = (f32[4,4,512]{0,2,1:T(8,128)}, f32[4,512,64,4]{2,3,1,0:T(4,128)}) fusion(pred[64]{0:T(512)(128)(4,1)S(1)} %iota_compare_fusion, bf16[64,4,64,512]{2,0,3,1:T(8,128)(2,1)} %copy.76, bf16[4,4,64,512]{2,0,3,1:T(4,128)(2,1)S(1)} %copy-done.2), kind=kOutput, calls=%fused_computation.1 | convolution fusion | flops 68673536 | bytes 19955776 | tf_op jit(solution)/shard_map/qhdc,khdc->qkhc/dot_general | solution.py:131
  344.9 1.3 broadcast_maximum_fusion
  346.2 30.0 %fusion.20 = f32[4,4,512]{0,2,1:T(8,128)S(1)} fusion(f32[4,4,512]{0,2,1:T(8,128)S(1)} %broadcast_maximum_fusion, f32[4,512,64,4]{2,3,1,0:T(4,128)} %get-tuple-element.11, pred[64]{0:T(512)(128)(4,1)S(1)} %iota_compare_fusion), kind=kLoop, calls=%fused_computation.35 | loop fusion | flops 2613248 | bytes 2162752 | tf_op jit(solution)/shard_map/reduce_sum | solution.py:138
  376.2 0.3 copy.70
  376.5 46.7 %copy.75 = bf16[64,4,64,512]{2,0,3,1:T(8,128)(2,1)} copy(bf16[64,4,64,512]{3,2,1,0:T(8,128)(2,1)} %get-tuple-element.3) | data formatting | bytes 33554432
  423.2 17.5 %fusion.11 = f32[4,512,64,4]{2,3,1,0:T(4,128)} fusion(bf16[64,4,64,512]{2,0,3,1:T(8,128)(2,1)} %copy.75, f32[4,512,64,4]{2,3,1,0:T(4,128)} %get-tuple-element.11, f32[4,4,512]{0,2,1:T(8,128)S(1)} %broadcast_maximum_fusion, pred[64]{0:T(512)(128)(4,1)S(1)} %iota_compare_fusion), kind=kOutput, calls=%fused_computation.23 | convolution fusion | flops 69730304 | bytes 21004352 | tf_op jit(solution)/shard_map/qkhc,khdc->qhdc/dot_general | solution.py:139
  440.6 3.5 copy.69
  444.2 0.3 fusion.6
  444.5 2.3 multiply_reduce_fusion
  446.7 64.6 %psum.7 = f32[]{:T(128)} all-reduce(f32[]{:T(128)} %get-tuple-element.12), channel_id=1, replica_groups=mesh['scene'=8,'frame'=16] {'scene','frame'}, use_global_device_ids=true, to_apply=%region_4.5 | all-reduce | flops 1 | bytes 8 | tf_op jit(solution)/shard_map/psum | solution.py:148
  (7 shorter events, 0.1 us)
Async XLA Ops:
  7.2 437.3 %copy-start = (bf16[256,256]{1,0:T(8,128)(2,1)S(1)}, bf16[256,256]{1,0:T(8,128)(2,1)}, u32[]{:S(2)}) copy-start(bf16[256,256]{1,0:T(8,128)(2,1)} %param.17) | copy-start | bytes 393220
  7.2 243.3 %all-gather.2.cloned.1.call-start = ((), (), s32[]{:S(2)}) async-start(), calls=%async_computation | async-start | bytes 35651584 | tf_op jit(solution)/shard_map/all_gather | solution.py:124
  10.5 2.9 copy-start.3
  16.0 5.0 copy-start.1
  30.8 5.8 %copy-start.4 = (bf16[3,256,256]{2,1,0:T(8,128)(2,1)S(1)}, bf16[3,256,256]{2,1,0:T(8,128)(2,1)}, u32[]{:S(2)}) copy-start(bf16[3,256,256]{2,1,0:T(8,128)(2,1)} %param.13) | copy-start | bytes 1179652
  31.2 8.9 %collective-permute-start = (bf16[1,256,512]{2,1,0:T(8,128)(2,1)S(1)}, bf16[1,256,512]{2,1,0:T(8,128)(2,1)S(1)}, u32[]{:S(2)}, u32[]{:S(2)}) collective-permute-start(bf16[1,256,512]{2,1,0:T(8,128)(2,1)S(1)} %get-tuple-element.5), channel_id=1, source_target_pairs={{0,1},{1,2},{2,3},{3,4},{4,5},{5,6},{6,7},{7,8},{8,9},{9,10},{10,1... | collective-permute-start | bytes 786440 | tf_op jit(solution)/shard_map/ppermute | solution.py:25
  35.1 8.8 %collective-permute-start.1 = (bf16[1,256,512]{2,1,0:T(8,128)(2,1)S(1)}, bf16[1,256,512]{2,1,0:T(8,128)(2,1)S(1)}, u32[]{:S(2)}, u32[]{:S(2)}) collective-permute-start(bf16[1,256,512]{2,1,0:T(8,128)(2,1)S(1)} %get-tuple-element.4), channel_id=1, source_target_pairs={{1,0},{2,1},{3,2},{4,3},{5,4},{6,5},{7,6},{8,7},{9,8},{10,9},{11,1... | collective-permute-start | bytes 786440 | tf_op jit(solution)/shard_map/ppermute | solution.py:27
  40.5 4.5 copy-start.5
  44.9 0.9 copy-start.6
  47.8 0.9 copy-start.7
  273.7 46.8 %copy-start.2 = (bf16[4,4,64,512]{2,0,3,1:T(4,128)(2,1)S(1)}, bf16[4,4,64,512]{2,0,3,1:T(4,128)(2,1)}, u32[]{:S(2)}) copy-start(bf16[4,4,64,512]{2,0,3,1:T(4,128)(2,1)} %copy.68) | copy-start | bytes 3145732
Sparse Core Ops, SparseCore 0:
  48.0 202.4 all-gather.1
